TPU v7x, 32 devices: a whole 2x2x4 slice. The times are simulated.
32 devices in a mesh: grp: 8 (over z, x), uly: 4 (over y, core).
Axes of the slice: x: 2, y: 2, z: 4, core: 2. Of those that a mesh axis runs over, the one named last changes fastest.
Arguments:
- tokens: bfloat16 [4096, 3072], P(('grp', 'uly')), may hold values from -60 to 60
- block_image: int32 [512], P(('grp', 'uly')), may hold values from 0 to 15, as said below
- dest_slot: int32 [512], P(('grp', 'uly')), may hold values from 0 to 15, as said below
- timestep: int32 [16], P('grp'), may hold values from 0 to 999
- txt_len: int32 [16], P('grp'), may hold values from 1 to 128
- mod_weight: bfloat16 [256, 9216], replicated, may hold values from -0.375 to 0.375
- qkv_weight: bfloat16 [3072, 6144], P('grp', 'uly'), may hold values from -0.109375 to 0.109375
- q_gain: float32 [128], replicated, may hold values from 1 to 2.5
- k_gain: float32 [128], replicated, may hold values from 1 to 2.5
- text_kv: bfloat16 [16, 128, 4096], P('grp', None, 'uly'), may hold values from -6 to 6
- out_weight: bfloat16 [2048, 3072], P(None, 'grp'), may hold values from -0.125 to 0.125
Outputs:
- update: bfloat16 [4096, 3072], P(('grp', 'uly'))
Inputs may be any that keep to these rules, and one draw needn't show every extreme that they name: `block_image`: image i belongs to group i // 2, and every image has at least 256 tokens. The blocks of one device name images of any one group at most 2 times, and some device does so 2 times. `dest_slot`: A block keeps its uly index and goes to group block_image // 2; every block slot of every device receives exactly one block. Along a group's positions, uly index times 16 plus slot, each image's blocks are contiguous and images come in increasing order.
All inputs are finite; a program needn't handle non-finite values.
Results may differ from a plain program's by a relative error of at most 0.015.
Values may be sent and summed in bfloat16 or wider, within the bound.
A program may use at most 128 MiB of HBM per device.

v0:
```python
import math

import jax
import jax.numpy as jnp
from jax import lax
from jax.sharding import PartitionSpec as P

HD = 128
TXT = 128
BLK = 8
IMG_GRP = 2


def layer_norm(values):
    mean = jnp.mean(values, axis=-1, keepdims=True)
    centred = values - mean
    spread = jnp.mean(centred * centred, axis=-1, keepdims=True)
    return centred * lax.rsqrt(spread + 1e-06)


def rms_scale(values, gain):
    return values * lax.rsqrt(jnp.mean(values * values, axis=-1, keepdims=True) + 1e-06) * gain


def modulation(timestep, mod_weight):
    half = mod_weight.shape[0] // 2
    freqs = jnp.exp(-math.log(10000.0) * jnp.arange(half, dtype=jnp.float32) / half)
    angles = timestep.astype(jnp.float32)[:, None] * freqs[None, :]
    embedded = jnp.concatenate([jnp.cos(angles), jnp.sin(angles)], axis=1)
    active = jax.nn.silu(embedded).astype(jnp.bfloat16)
    return jnp.dot(active, mod_weight, preferred_element_type=jnp.float32)


def select_rows(mods, owner):
    onehot = (owner[:, None] == jnp.arange(mods.shape[0], dtype=jnp.int32)[None, :]).astype(
        jnp.float32
    )
    return jnp.dot(onehot, mods, precision=lax.Precision.HIGHEST)


def tile_terms(query, q_owner, keys, values, k_owner, k_live):
    scores = jnp.einsum(
        "qhd,khd->hqk", query, keys, preferred_element_type=jnp.float32
    ) * query.shape[-1] ** (-0.5)
    match = (q_owner[:, None] == k_owner[None, :]) & k_live[None, :]
    weights = jnp.where(match[None], jnp.exp(scores), 0.0)
    total = jnp.sum(weights, axis=2)
    summed = jnp.einsum(
        "hqk,khd->qhd", weights.astype(jnp.bfloat16), values, preferred_element_type=jnp.float32
    )
    return (total, summed)


def body(
    tokens,
    block_image,
    dest_slot,
    timestep,
    txt_len,
    mod_weight,
    qkv_weight,
    q_gain,
    k_gain,
    text_kv,
    out_weight,
):
    groups = lax.axis_size("grp")
    width = tokens.shape[1]
    blocks = block_image.shape[0]
    capacity = (blocks + groups - 1) // groups
    target = block_image // IMG_GRP
    own_image = block_image % IMG_GRP
    hits = (target[:, None] == jnp.arange(groups, dtype=jnp.int32)[None, :]).astype(jnp.int32)
    before = jnp.sum((jnp.cumsum(hits, axis=0) - hits) * hits, axis=1)
    place = target * capacity + before
    rows = tokens.reshape(blocks, BLK * width)
    outgoing = jnp.zeros((groups * capacity, BLK * width), jnp.bfloat16).at[place].set(rows)
    labels = jnp.stack([dest_slot, own_image], axis=1).astype(jnp.bfloat16)
    tags = jnp.full((groups * capacity, 2), -1.0, jnp.bfloat16).at[place].set(labels)
    arrived, arrived_tags = (
        lax.all_to_all(
            outgoing.reshape(groups, capacity, BLK * width),
            "grp",
            split_axis=0,
            concat_axis=0,
            tiled=True,
        ),
        lax.all_to_all(
            tags.reshape(groups, capacity, 2), "grp", split_axis=0, concat_axis=0, tiled=True
        ),
    )
    arrived_tags = arrived_tags.reshape(groups * capacity, 2).astype(jnp.int32)
    slot_of = jnp.where(arrived_tags[:, 0] < 0, blocks, arrived_tags[:, 0])
    placed = (
        jnp.zeros((blocks + 1, BLK * width), jnp.bfloat16)
        .at[slot_of]
        .set(arrived.reshape(groups * capacity, BLK * width))[:blocks]
    )
    block_owner = jnp.zeros((blocks + 1,), jnp.int32).at[slot_of].set(arrived_tags[:, 1])[:blocks]
    mods = modulation(timestep, mod_weight)
    picked = select_rows(mods, jnp.repeat(block_owner, BLK))
    shift = picked[:, :width]
    scale = picked[:, width : 2 * width]
    gate = picked[:, 2 * width :]
    local_rows = placed.reshape(blocks * BLK, width)
    hidden = (layer_norm(local_rows.astype(jnp.float32)) * (1.0 + scale) + shift).astype(
        jnp.bfloat16
    )
    everyone, owners = (
        lax.all_gather(hidden, "uly", axis=0, tiled=True),
        lax.all_gather(block_owner.astype(jnp.bfloat16), "uly", axis=0, tiled=True),
    )
    weights = lax.all_gather(qkv_weight, "grp", axis=0, tiled=True)
    local_heads = weights.shape[1] // (3 * HD)
    projected = jnp.dot(everyone, weights, preferred_element_type=jnp.float32).reshape(
        -1, local_heads, 3, HD
    )
    query = rms_scale(projected[:, :, 0], q_gain).astype(jnp.bfloat16)
    keys = rms_scale(projected[:, :, 1], k_gain).astype(jnp.bfloat16)
    values = projected[:, :, 2].astype(jnp.bfloat16)
    text = text_kv.reshape(IMG_GRP, TXT, local_heads, 2, HD)
    text_key = (
        rms_scale(text[:, :, :, 0].astype(jnp.float32), k_gain)
        .astype(jnp.bfloat16)
        .reshape(IMG_GRP * TXT, local_heads, HD)
    )
    text_value = text[:, :, :, 1].reshape(IMG_GRP * TXT, local_heads, HD)
    owner = jnp.repeat(owners.astype(jnp.int32), BLK)
    text_owner = jnp.repeat(jnp.arange(IMG_GRP, dtype=jnp.int32), TXT)
    text_live = jnp.tile(jnp.arange(TXT, dtype=jnp.int32), IMG_GRP) < jnp.repeat(txt_len, TXT)
    group_tokens = owner.shape[0]
    tile = 512
    count = group_tokens // tile
    query_tiles = (query.reshape(count, tile, local_heads, HD), owner.reshape(count, tile))
    all_keys = jnp.concatenate([keys, text_key], axis=0)
    all_values = jnp.concatenate([values, text_value], axis=0)
    k_owner = jnp.concatenate([owner, text_owner])
    k_live = jnp.concatenate([jnp.ones(owner.shape, bool), text_live])

    def dense_tile(pair):
        total, summed = tile_terms(pair[0], pair[1], all_keys, all_values, k_owner, k_live)
        return (summed / total.T[:, :, None]).astype(jnp.bfloat16)

    mixed = lax.map(dense_tile, query_tiles)
    mixed = mixed.reshape(group_tokens, local_heads * HD)
    gathered = lax.all_to_all(mixed, "uly", split_axis=0, concat_axis=1, tiled=True)
    projection = jnp.dot(
        gathered,
        lax.all_gather(out_weight, "grp", axis=1, tiled=True),
        preferred_element_type=jnp.float32,
    )
    return (gate * projection).astype(jnp.bfloat16)


def solution(mesh):
    return jax.shard_map(
        body,
        mesh=mesh,
        in_specs=(
            P(("grp", "uly"), None),
            P(("grp", "uly")),
            P(("grp", "uly")),
            P("grp"),
            P("grp"),
            P(),
            P("grp", "uly"),
            P(),
            P(),
            P("grp", None, "uly"),
            P(None, "grp"),
        ),
        out_specs=P(("grp", "uly"), None),
        check_vma=False,
    )
```

profile of v0, /device:TPU:9, one launch (start us, length us, event | category | flops | bytes accessed | tf_op | source)
XLA Modules:
  0.0 409.1 jit_solution(7401317636670699244)
XLA Ops:
  6.5 0.7 fusion.42
  7.2 0.1 fusion.34
  7.3 0.2 select_reduce_fusion
  7.5 0.7 convert_bitcast_fusion
  8.2 0.1 copy.37
  8.3 0.6 scatter_custom_fusion
  8.9 0.7 copy.39
  9.6 5.7 %all-to-all-start = ((bf16[8,2,2]{1,2,0:T(2,128)(2,1)}), bf16[8,2,2]{1,2,0:T(2,128)(2,1)S(1)}, u32[]{:S(2)}, u32[]{:S(2)}) async-start(bf16[8,2,2]{1,2,0:T(2,128)(2,1)} %copy.39), calls=%async_computation | async-start | bytes 8192 | tf_op jit(solution)/shard_map/all_to_all | solution.py:88
  15.3 1.5 reshape.180
  16.8 1.8 scatter_custom_fusion.2
  18.7 1.4 reshape.152
  20.1 5.4 %all-to-all-start.1 = ((bf16[8,2,24576]{2,1,0:T(2,128)(2,1)}), bf16[8,2,24576]{2,1,0:T(2,128)(2,1)S(1)}, u32[]{:S(2)}, u32[]{:S(2)}) async-start(bf16[8,2,24576]{2,1,0:T(2,128)(2,1)} %reshape.152), calls=%async_computation.1 | async-start | bytes 1572864 | tf_op jit(solution)/shard_map/all_to_all | solution.py:81
  25.5 0.1 multiply_cosine_fusion
  25.6 3.1 fusion.38
  28.7 0.1 copy.40
  28.8 0.1 copy.41
  28.9 0.1 reshape.157
  29.0 0.6 scatter_custom_fusion.1
  29.6 0.1 broadcast_in_dim.75
  29.7 0.1 eq.59
  29.8 4.2 %fusion.32 = f32[128,9216]{1,0:T(8,128)} fusion(f32[2,9216]{1,0:T(2,128)S(1)} %fusion.38, s32[128]{0:T(128)S(1)} %eq.59), kind=kOutput, calls=%fused_computation.49 | convolution fusion | flops 28311808 | bytes 4792832 | tf_op jit(solution)/shard_map/dot_general | solution.py:38
  34.0 7.8 %all-to-all-done.1 = bf16[8,2,24576]{2,1,0:T(2,128)(2,1)S(1)} async-done(((bf16[8,2,24576]{2,1,0:T(2,128)(2,1)}), bf16[8,2,24576]{2,1,0:T(2,128)(2,1)S(1)}, u32[]{:S(2)}, u32[]{:S(2)}) %all-to-all-start.1) | async-done | bytes 786464 | tf_op jit(solution)/shard_map/all_to_all | solution.py:81
  41.9 0.3 reshape.188
  42.2 2.0 scatter_custom_fusion.3
  44.2 0.1 slice_convert_fusion
  44.3 0.3 reshape.158
  44.6 0.2 reduce_sum.65
  44.7 0.3 multiply_reduce_fusion
  45.1 3.3 fusion.8
  48.4 0.0 all-gather.4.cloned.1.call-update
  48.4 0.0 all-gather.6.cloned.1.call-start
  48.4 0.7 all-gather.6.cloned.1.call-update
  49.2 0.0 all-gather.8.cloned.1.call-start
  49.2 0.7 all-gather.8.cloned.1.call-update
  49.9 0.4 reshape.155
  50.3 0.7 fusion.52
  51.0 0.2 multiply_reduce_fusion.2
  51.3 0.1 copy.57
  51.4 0.2 copy.56
  51.6 0.6 dynamic-slice.1
  52.8 0.1 compare_bitcast_fusion
  52.9 0.2 multiply_convert_fusion.2
  53.1 0.2 dynamic-update-slice
  53.4 8.5 %all-reduce.1 = bf16[64]{0:T(256)(128)(2,1)S(1)} all-reduce(bf16[64]{0:T(256)(128)(2,1)S(1)} %dynamic-update-slice), channel_id=1, replica_groups=mesh['grp'=8,'uly'=4] {'uly'}, use_global_device_ids=true, to_apply=%add.1 | all-reduce | flops 64 | bytes 256
  61.9 0.1 broadcast_in_dim.78
  62.0 0.1 eq.63
  62.1 0.3 compare_and_fusion
  62.4 18.0 %all-gather.4.cloned.1.call-done = bf16[512,3072]{1,0:T(8,128)(2,1)} async-done(((bf16[128,3072]{1,0:T(8,128)(2,1)}), bf16[512,3072]{1,0:T(8,128)(2,1)}) %all-gather.4.cloned.1.call-update) | async-done | bytes 3145744 | tf_op jit(solution)/shard_map/all_gather | solution.py:110
  80.4 137.6 %all-gather.6.cloned.1.call-done = bf16[3072,1536]{1,0:T(8,128)(2,1)} async-done(((bf16[384,1536]{1,0:T(8,128)(2,1)}), bf16[3072,1536]{1,0:T(8,128)(2,1)}) %all-gather.6.cloned.1.call-update) | async-done | bytes 9437200 | tf_op jit(solution)/shard_map/all_gather | solution.py:113
  218.0 8.7 %fusion.53 = f32[512,1536]{0,1:T(8,128)S(1)} fusion(bf16[512,3072]{1,0:T(8,128)(2,1)} %all-gather.4.cloned.1.call-done, bf16[3072,1536]{1,0:T(8,128)(2,1)} %all-gather.6.cloned.1.call-done), kind=kOutput, calls=%fused_computation.97 | convolution fusion | flops 4831838208 | bytes 15728640 | tf_op jit(solution)/shard_map/dot_general | solution.py:115
  226.7 1.7 copy-done
  228.3 0.1 slice.57
  228.4 0.3 copy.54
  228.8 0.4 fusion.13
  229.1 1.5 multiply_reduce_fusion.1
  230.7 1.3 fusion.27
  232.0 0.3 fusion.15
  232.4 3.4 fusion
  235.8 1.5 divide_convert_fusion
  237.2 0.1 all_to_all.22
  237.4 0.1 copy.48
  237.5 11.8 %all_to_all.29 = bf16[4,128,512]{1,2,0:T(8,128)(2,1)S(1)} all-to-all(bf16[4,128,512]{1,2,0:T(8,128)(2,1)S(1)} %copy.48), channel_id=1, replica_groups=mesh['grp'=8,'uly'=4] {'uly'}, dimensions={0} | all-to-all | bytes 1048576 | tf_op jit(solution)/shard_map/all_to_all | solution.py:146
  249.2 145.7 %all-gather.8.cloned.1.call-done = bf16[2048,3072]{1,0:T(8,128)(2,1)} async-done(((bf16[2048,384]{1,0:T(8,128)(2,1)}), bf16[2048,3072]{1,0:T(8,128)(2,1)}) %all-gather.8.cloned.1.call-update) | async-done | bytes 12582928 | tf_op jit(solution)/shard_map/all_gather | solution.py:149
  394.9 7.7 %fusion.2 = bf16[128,3072]{1,0:T(8,128)(2,1)} fusion(bf16[128,2048]{0,1:T(8,128)(2,1)S(1)} %bitcast.62, bf16[2048,3072]{1,0:T(8,128)(2,1)} %all-gather.8.cloned.1.call-done, f32[128,9216]{1,0:T(8,128)} %fusion.32), kind=kOutput, calls=%fused_computation.8 | convolution fusion | flops 1611399168 | bytes 15466496 | tf_op jit(solution)/shard_map/dot_general | solution.py:147
  (35 shorter events, 0.2 us)
Async XLA Ops:
  6.5 19.0 %copy-start.3 = (s32[2]{0:T(128)S(1)}, s32[2]{0:T(128)}, u32[]{:S(2)}) copy-start(s32[2]{0:T(128)} %param.14) | copy-start | bytes 28
  9.6 10.4 %all-to-all-start = ((bf16[8,2,2]{1,2,0:T(2,128)(2,1)}), bf16[8,2,2]{1,2,0:T(2,128)(2,1)S(1)}, u32[]{:S(2)}, u32[]{:S(2)}) async-start(bf16[8,2,2]{1,2,0:T(2,128)(2,1)} %copy.39), calls=%async_computation | async-start | bytes 8192 | tf_op jit(solution)/shard_map/all_to_all | solution.py:88
  20.1 21.8 %all-to-all-start.1 = ((bf16[8,2,24576]{2,1,0:T(2,128)(2,1)}), bf16[8,2,24576]{2,1,0:T(2,128)(2,1)S(1)}, u32[]{:S(2)}, u32[]{:S(2)}) async-start(bf16[8,2,24576]{2,1,0:T(2,128)(2,1)} %reshape.152), calls=%async_computation.1 | async-start | bytes 1572864 | tf_op jit(solution)/shard_map/all_to_all | solution.py:81
  25.5 54.9 %all-gather.4.cloned.1.call-start = ((), (), s32[]{:S(2)}) async-start(), calls=%async_computation.3 | async-start | bytes 3932160 | tf_op jit(solution)/shard_map/all_gather | solution.py:110
  48.4 1.6 copy-start.1
  48.4 169.6 %all-gather.6.cloned.1.call-start = ((), (), s32[]{:S(2)}) async-start(), calls=%async_computation.4 | async-start | bytes 10616832 | tf_op jit(solution)/shard_map/all_gather | solution.py:113
  49.1 2.4 copy-start.6
  49.2 3.6 copy-start.4
  49.2 345.7 %all-gather.8.cloned.1.call-start = ((), (), s32[]{:S(2)}) async-start(), calls=%async_computation.5 | async-start | bytes 14155776 | tf_op jit(solution)/shard_map/all_gather | solution.py:149
  49.9 3.0 copy-start.2
  226.7 1.7 copy-start
  228.4 4.0 copy-start.5
Sparse Core Ops, SparseCore 0:
  48.5 31.8 all-gather.3
  82.6 135.3 all-gather.5
  220.1 174.7 all-gather.7
where the time goes:
time: 413 us; the launch traced here: 409 us
  waiting for transfers between devices  310 us (75%)
  matrix products  28.5 us (7%)
  blocking collectives  20.3 us (5%)
  local copies, waits for them, and re-layouts  15.8 us (4%)
  between operations  14 us (3%)
  starting transfers between devices  11.2 us (3%)
  other arithmetic  8.81 us (2%)
    all_gather x1, waiting for transfers between devices, body(): lax.all_gather(out_weight, 'grp', axis=1, tiled=True)  146 us
    all_gather x1, waiting for transfers between devices, body(): weights = lax.all_gather(qkv_weight, 'grp', axis=0, tiled=True)  138 us
    all_gather x1, waiting for transfers between devices, body(): lax.all_gather(hidden, 'uly', axis=0, tiled=True)  18 us
    all_to_all x1, blocking collectives, body(): lax.all_to_all(mixed, 'uly', split_axis=0, concat_axis=1, tiled=True)  11.8 us
    dot_general x1, matrix products, body(): jnp.dot(everyone, weights, preferred_element_type=jnp.float32)  8.65 us
    unnamed x1, blocking collectives  8.52 us
  transfers between devices with their start and end apart: 5, of which 4 were waited for; matrix products, arithmetic and copies ran while one was open for 8% of the time, Pallas kernels for 0%

commit v1 on v0

v1 whole, which is shorter than its diff:
```python
import functools
import math

import jax
import jax.numpy as jnp
from jax import lax
from jax.experimental import pallas as pl
from jax.experimental.pallas import tpu as pltpu
from jax.sharding import PartitionSpec as P

HD = 128
TXT = 128
BLK = 8
IMG_GRP = 2


def layer_norm(values):
    mean = jnp.mean(values, axis=-1, keepdims=True)
    centred = values - mean
    spread = jnp.mean(centred * centred, axis=-1, keepdims=True)
    return centred * lax.rsqrt(spread + 1e-06)


def rms_scale(values, gain):
    return values * lax.rsqrt(jnp.mean(values * values, axis=-1, keepdims=True) + 1e-06) * gain


def modulation(timestep, mod_weight):
    half = mod_weight.shape[0] // 2
    freqs = jnp.exp(-math.log(10000.0) * jnp.arange(half, dtype=jnp.float32) / half)
    angles = timestep.astype(jnp.float32)[:, None] * freqs[None, :]
    embedded = jnp.concatenate([jnp.cos(angles), jnp.sin(angles)], axis=1)
    active = jax.nn.silu(embedded).astype(jnp.bfloat16)
    return jnp.dot(active, mod_weight, preferred_element_type=jnp.float32)


def select_rows(mods, owner):
    onehot = (owner[:, None] == jnp.arange(mods.shape[0], dtype=jnp.int32)[None, :]).astype(
        jnp.float32
    )
    return jnp.dot(onehot, mods, precision=lax.Precision.HIGHEST)


def tile_terms(query, q_owner, keys, values, k_owner, k_live):
    scores = jnp.einsum(
        "qhd,khd->hqk", query, keys, preferred_element_type=jnp.float32
    ) * query.shape[-1] ** (-0.5)
    match = (q_owner[:, None] == k_owner[None, :]) & k_live[None, :]
    weights = jnp.where(match[None], jnp.exp(scores), 0.0)
    total = jnp.sum(weights, axis=2)
    summed = jnp.einsum(
        "hqk,khd->qhd", weights.astype(jnp.bfloat16), values, preferred_element_type=jnp.float32
    )
    return (total, summed)


MESH = pl.DeviceIdType.MESH
CHUNKS = 2


def fused_kernel(
    groups,
    lanes,
    pad,
    tokens_ref,
    place_ref,
    tags_ref,
    mods_ref,
    weight_ref,
    acc_ref,
    count_ref,
    out_blocks,
    in_blocks,
    in_tags,
    hidden_all,
    weight_all,
    counts_all,
    block_send,
    block_recv,
    tag_send,
    tag_recv,
    hid_send,
    hid_recv,
    cnt_send,
    cnt_recv,
    ring_send,
    ring_recv,
):
    g = lax.axis_index("grp")
    u = lax.axis_index("uly")
    rows, width = tokens_ref.shape
    depth, columns = weight_ref.shape
    half = columns // 2
    piece = depth // CHUNKS
    span = groups * pad

    def group_at(position):
        high = position // (groups // 2)
        return (1 - high) * 2 * position + high * (2 * (groups - 1 - position) + 1)

    odd = g % 2
    position = (1 - odd) * (g // 2) + odd * (groups - 1 - g // 2)
    ahead = group_at((position + 1) % groups)
    behind = group_at((position + groups - 1) % groups)

    barrier = pltpu.get_barrier_semaphore()
    for k in range(1, groups):
        pl.semaphore_signal(
            barrier, inc=1, device_id=((g + k) % groups, u), device_id_type=MESH
        )
    for k in range(1, lanes):
        pl.semaphore_signal(barrier, inc=1, device_id=(g, (u + k) % lanes), device_id_type=MESH)

    spot = lax.broadcasted_iota(jnp.int32, (span, rows), 0)
    pick = jnp.where(spot == place_ref[0:1, :], 1.0, 0.0).astype(jnp.bfloat16)
    sorted_rows = jnp.dot(pick, tokens_ref[...], preferred_element_type=jnp.float32)
    out_blocks[...] = sorted_rows.astype(jnp.bfloat16).reshape(groups, pad, width)
    in_blocks[g] = out_blocks[g]
    in_tags[g] = tags_ref[g]

    pl.semaphore_wait(barrier, groups + lanes - 2)

    def ring_copy(way, chunk, step):
        if way == 0:
            owner = group_at((position + groups - step) % groups)
            target = ahead
        else:
            owner = group_at((position + step) % groups)
            target = behind
        place = weight_all.at[
            owner, pl.ds(chunk * piece, piece), pl.ds(way * half, half)
        ]
        return pltpu.make_async_remote_copy(
            src_ref=place,
            dst_ref=place,
            send_sem=ring_send.at[way, chunk, step],
            recv_sem=ring_recv.at[way, chunk, step],
            device_id=(target, u),
            device_id_type=MESH,
        )

    def block_copy(k):
        peer = (g + k) % groups
        return pltpu.make_async_remote_copy(
            src_ref=out_blocks.at[peer],
            dst_ref=in_blocks.at[g],
            send_sem=block_send.at[k],
            recv_sem=block_recv.at[k],
            device_id=(peer, u),
            device_id_type=MESH,
        )

    def tag_copy(k):
        peer = (g + k) % groups
        return pltpu.make_async_remote_copy(
            src_ref=tags_ref.at[peer],
            dst_ref=in_tags.at[g],
            send_sem=tag_send.at[k],
            recv_sem=tag_recv.at[k],
            device_id=(peer, u),
            device_id_type=MESH,
        )

    for k in range(1, groups):
        tag_copy(k).start()
        block_copy(k).start()
    weight_all[g] = weight_ref[...]
    for chunk in range(CHUNKS):
        for way in range(2):
            ring_copy(way, chunk, 0).start()
    for k in range(1, groups):
        tag_copy(k).wait()
        block_copy(k).wait()

    tag = jnp.max(in_tags[...], axis=0)[0:1, :]
    slot = lax.broadcasted_iota(jnp.int32, (rows, span), 0)
    match = slot == (tag >> 1)
    owner_col = jnp.sum(
        jnp.where(match, (tag & 1).astype(jnp.float32), 0.0), axis=1, keepdims=True
    )
    values = jnp.dot(
        jnp.where(match, 1.0, 0.0).astype(jnp.bfloat16),
        in_blocks[...].reshape(span, width),
        preferred_element_type=jnp.float32,
    )
    mods = mods_ref[...]
    first = owner_col < 0.5
    shift = jnp.where(first, mods[0:1, :width], mods[1:2, :width])
    scale = jnp.where(first, mods[0:1, width : 2 * width], mods[1:2, width : 2 * width])
    hidden = (layer_norm(values) * (1.0 + scale) + shift).astype(jnp.bfloat16)
    mine = pl.ds(pl.multiple_of(u * rows, rows), rows)
    for part in range(groups):
        hidden_all[part, mine, :] = hidden[:, part * depth : (part + 1) * depth]
    counts_all[u] = jnp.broadcast_to(
        jnp.sum(jnp.where(first, 1.0, 0.0), axis=0, keepdims=True), counts_all.shape[1:]
    )

    def hidden_copy(k):
        return pltpu.make_async_remote_copy(
            src_ref=hidden_all.at[:, mine, :],
            dst_ref=hidden_all.at[:, mine, :],
            send_sem=hid_send.at[k],
            recv_sem=hid_recv.at[k],
            device_id=(g, (u + k) % lanes),
            device_id_type=MESH,
        )

    def count_copy(k):
        return pltpu.make_async_remote_copy(
            src_ref=counts_all.at[u],
            dst_ref=counts_all.at[u],
            send_sem=cnt_send.at[k],
            recv_sem=cnt_recv.at[k],
            device_id=(g, (u + k) % lanes),
            device_id_type=MESH,
        )

    for k in range(1, lanes):
        hidden_copy(k).start()
        count_copy(k).start()

    def pass_on(step):
        for chunk in range(CHUNKS):
            for way in range(2):
                ring_copy(way, chunk, step).wait()

                @pl.when(step < groups - 2)
                def _():
                    ring_copy(way, chunk, step + 1).start()

    def add_block(step):
        left = group_at((position + groups - step) % groups)
        right = group_at((position + step) % groups)
        acc_ref[:, :half] += jnp.dot(
            hidden_all[left], weight_all[left, :, :half], preferred_element_type=jnp.float32
        )
        acc_ref[:, half:] += jnp.dot(
            hidden_all[right], weight_all[right, :, half:], preferred_element_type=jnp.float32
        )

    early = groups // 2 - 1

    def forward_only(step, carry):
        pass_on(step)
        return carry

    lax.fori_loop(0, early, forward_only, 0)
    acc_ref[...] = jnp.zeros_like(acc_ref)
    for k in range(1, lanes):
        hidden_copy(k).wait()
        count_copy(k).wait()
    count_ref[...] = jnp.sum(counts_all[...], axis=0)

    def held(step, carry):
        add_block(step)
        return carry

    def arriving(step, carry):
        pass_on(step)
        add_block(step + 1)
        return carry

    lax.fori_loop(0, early + 1, held, 0)
    lax.fori_loop(early, groups - 1, arriving, 0)


def project(tokens, place, tags, mods, qkv_weight, pad):
    groups = lax.axis_size("grp")
    lanes = lax.axis_size("uly")
    rows, width = tokens.shape
    depth, columns = qkv_weight.shape
    vmem = pl.BlockSpec(memory_space=pltpu.VMEM)
    dma = pltpu.SemaphoreType.DMA
    return pl.pallas_call(
        functools.partial(fused_kernel, groups, lanes, pad),
        out_shape=(
            jax.ShapeDtypeStruct((rows * lanes, columns), jnp.float32),
            jax.ShapeDtypeStruct((8, 128), jnp.float32),
        ),
        in_specs=[vmem] * 5,
        out_specs=(vmem, vmem),
        scratch_shapes=[
            pltpu.VMEM((groups, pad, width), jnp.bfloat16),
            pltpu.VMEM((groups, pad, width), jnp.bfloat16),
            pltpu.VMEM((groups, 8, groups * pad), jnp.int32),
            pltpu.VMEM((groups, rows * lanes, depth), jnp.bfloat16),
            pltpu.VMEM((groups, depth, columns), jnp.bfloat16),
            pltpu.VMEM((lanes, 8, 128), jnp.float32),
            dma((groups,)),
            dma((groups,)),
            dma((groups,)),
            dma((groups,)),
            dma((lanes,)),
            dma((lanes,)),
            dma((lanes,)),
            dma((lanes,)),
            dma((2, CHUNKS, groups)),
            dma((2, CHUNKS, groups)),
        ],
        compiler_params=pltpu.CompilerParams(
            collective_id=0, has_side_effects=True, vmem_limit_bytes=48 * 1024 * 1024
        ),
        cost_estimate=pl.CostEstimate(
            flops=2 * rows * lanes * width * columns,
            bytes_accessed=200 * 1024 * 1024,
            transcendentals=0,
        ),
    )(tokens, place, tags, mods, qkv_weight)


def output_kernel(lanes, mixed_ref, weight_ref, out_ref, sending, landing, send_sem, recv_sem):
    g = lax.axis_index("grp")
    u = lax.axis_index("uly")
    rows = out_ref.shape[0]
    barrier = pltpu.get_barrier_semaphore()
    for k in range(1, lanes):
        pl.semaphore_signal(barrier, inc=1, device_id=(g, (u + k) % lanes), device_id_type=MESH)
    pl.semaphore_wait(barrier, lanes - 1)

    def part(index):
        return jnp.dot(
            mixed_ref[pl.ds(pl.multiple_of(index * rows, rows), rows), :],
            weight_ref[...],
            preferred_element_type=jnp.float32,
        )

    def copy(k):
        return pltpu.make_async_remote_copy(
            src_ref=sending.at[k - 1],
            dst_ref=landing.at[k - 1],
            send_sem=send_sem.at[k - 1],
            recv_sem=recv_sem.at[k - 1],
            device_id=(g, (u + k) % lanes),
            device_id_type=MESH,
        )

    order = sorted(range(1, lanes), key=lambda k: abs(k - lanes // 2))
    for k in order:
        sending[k - 1] = part((u + k) % lanes).astype(jnp.bfloat16)
        copy(k).start()
    out_ref[...] = part(u)
    for k in order:
        copy(k).wait()
        out_ref[...] += landing[k - 1].astype(jnp.float32)


def output_projection(mixed, weight):
    lanes = lax.axis_size("uly")
    rows = mixed.shape[0] // lanes
    width = weight.shape[1]
    vmem = pl.BlockSpec(memory_space=pltpu.VMEM)
    return pl.pallas_call(
        functools.partial(output_kernel, lanes),
        out_shape=jax.ShapeDtypeStruct((rows, width), jnp.float32),
        in_specs=[vmem] * 2,
        out_specs=vmem,
        scratch_shapes=[
            pltpu.VMEM((lanes - 1, rows, width), jnp.bfloat16),
            pltpu.VMEM((lanes - 1, rows, width), jnp.bfloat16),
            pltpu.SemaphoreType.DMA((lanes - 1,)),
            pltpu.SemaphoreType.DMA((lanes - 1,)),
        ],
        compiler_params=pltpu.CompilerParams(
            collective_id=1, has_side_effects=True, vmem_limit_bytes=40 * 1024 * 1024
        ),
    )(mixed, weight)


def body(
    tokens,
    block_image,
    dest_slot,
    timestep,
    txt_len,
    mod_weight,
    qkv_weight,
    q_gain,
    k_gain,
    text_kv,
    out_weight,
):
    groups = lax.axis_size("grp")
    lanes = lax.axis_size("uly")
    rows, width = tokens.shape
    blocks = block_image.shape[0]
    capacity = (blocks + groups - 1) // groups
    pad = (capacity * BLK + 15) // 16 * 16
    span = groups * pad
    g = lax.axis_index("grp")
    u = lax.axis_index("uly")
    target = block_image // IMG_GRP
    own_image = block_image % IMG_GRP
    index = jnp.arange(blocks, dtype=jnp.int32)
    before = jnp.sum(
        ((target[:, None] == target[None, :]) & (index[None, :] < index[:, None])).astype(jnp.int32),
        axis=1,
    )
    row = jnp.arange(BLK, dtype=jnp.int32)
    place = ((target * pad + before * BLK)[:, None] + row[None, :]).reshape(rows)
    code = ((dest_slot[:, None] * BLK + row[None, :]) * 2 + own_image[:, None]).reshape(rows)
    hits = place[None, :] == jnp.arange(span, dtype=jnp.int32)[:, None]
    codes = (jnp.sum(jnp.where(hits, code[None, :] + 1, 0), axis=1) - 1).reshape(groups, pad)
    own_lane = jnp.arange(span, dtype=jnp.int32) // pad == g
    tags = jnp.where(own_lane[None, :], jnp.tile(codes, (1, groups)), -1)
    tags = jnp.broadcast_to(tags[:, None, :], (groups, 8, span))
    places = jnp.broadcast_to(place[None, :], (8, rows))

    share = out_weight.shape[0] // lanes
    own_rows = lax.dynamic_slice_in_dim(out_weight, u * share, share, axis=0)
    out_rows = lax.all_gather(own_rows, "grp", axis=1, tiled=True)

    mods = modulation(timestep, mod_weight)
    projected, count = project(tokens, places, tags, mods, qkv_weight, pad)
    local_heads = qkv_weight.shape[1] // (3 * HD)
    group_tokens = rows * lanes
    projected = projected.reshape(-1, local_heads, 3, HD)
    query = rms_scale(projected[:, :, 0], q_gain).astype(jnp.bfloat16)
    keys = rms_scale(projected[:, :, 1], k_gain).astype(jnp.bfloat16)
    values = projected[:, :, 2].astype(jnp.bfloat16)
    text = text_kv.reshape(IMG_GRP, TXT, local_heads, 2, HD)
    text_key = (
        rms_scale(text[:, :, :, 0].astype(jnp.float32), k_gain)
        .astype(jnp.bfloat16)
        .reshape(IMG_GRP * TXT, local_heads, HD)
    )
    text_value = text[:, :, :, 1].reshape(IMG_GRP * TXT, local_heads, HD)
    first_count = count[0, 0].astype(jnp.int32)
    owner = (jnp.arange(group_tokens, dtype=jnp.int32) >= first_count).astype(jnp.int32)
    text_owner = jnp.repeat(jnp.arange(IMG_GRP, dtype=jnp.int32), TXT)
    text_live = jnp.tile(jnp.arange(TXT, dtype=jnp.int32), IMG_GRP) < jnp.repeat(txt_len, TXT)
    all_keys = jnp.concatenate([keys, text_key], axis=0)
    all_values = jnp.concatenate([values, text_value], axis=0)
    k_owner = jnp.concatenate([owner, text_owner])
    k_live = jnp.concatenate([jnp.ones(owner.shape, bool), text_live])
    total, summed = tile_terms(query, owner, all_keys, all_values, k_owner, k_live)
    mixed = (summed / total.T[:, :, None]).astype(jnp.bfloat16)
    mixed = mixed.reshape(group_tokens, local_heads * HD)
    projection = output_projection(mixed, out_rows)
    own_first = (u * rows + jnp.arange(rows, dtype=jnp.int32)) < first_count
    gate = jnp.where(own_first[:, None], mods[0:1, 2 * width :], mods[1:2, 2 * width :])
    return (gate * projection).astype(jnp.bfloat16)


def solution(mesh):
    return jax.shard_map(
        body,
        mesh=mesh,
        in_specs=(
            P(("grp", "uly"), None),
            P(("grp", "uly")),
            P(("grp", "uly")),
            P("grp"),
            P("grp"),
            P(),
            P("grp", "uly"),
            P(),
            P(),
            P("grp", None, "uly"),
            P(None, "grp"),
        ),
        out_specs=P(("grp", "uly"), None),
        check_vma=False,
    )
```

time: 413 us -> 236 us (0.57)
  waiting for transfers between devices: 310 us -> 0.04 us
  Pallas kernels: 0 us -> 188 us
  matrix products: 28.5 us -> 6.63 us
  blocking collectives: 20.3 us -> 0 us
  starting transfers between devices: 11.2 us -> 0.01 us
    all_gather x3 -> x1, waiting for transfers between devices: 301 us -> 0.02 us  [body(): out_rows = lax.all_gather(own_rows, 'grp', axis=1, tiled=True)]
    pallas_call x0 -> x2, Pallas kernels: none -> 188 us  [the longest x1 150 us: project(): pl.pallas_call(functools.partial(fused_kernel, groups, lanes, pad), out_s...]
    dot_general x3 -> x0, matrix products: 20.6 us -> none  [the longest x1 8.65 us: body(): jnp.dot(everyone, weights, preferred_element_type=jnp.float32)]
    all_to_all x1 -> x0, blocking collectives: 11.8 us -> none  [body(): lax.all_to_all(mixed, 'uly', split_axis=0, concat_axis=1, tiled=True)]
    all_to_all x2 -> x0, starting transfers between devices: 11.1 us -> none  [the longest x1 5.69 us: body(): lax.all_to_all(tags.reshape(groups, capacity, 2), 'grp', split_axis=0, co...]
    unnamed x1 -> x0, blocking collectives: 8.52 us -> none
    all_to_all x2 -> x0, waiting for transfers between devices: 7.85 us -> none  [the longest x1 7.85 us: body(): lax.all_to_all(outgoing.reshape(groups, capacity, BLK * width), 'grp', sp...]
    unnamed x20 -> x27, local copies, waits for them, and re-layouts: 2.95 us -> 8.15 us
  transfers between devices with their start and end apart: 5 -> 1, of which waited for: 4 -> 0; matrix products, arithmetic and copies ran while one was open for 8% -> 11% of each run, Pallas kernels for 0% -> 64%
where the time goes in v1:
time: 236 us; the launch traced here: 235 us
  Pallas kernels  188 us (80%)
  local copies, waits for them, and re-layouts  19.9 us (8%)
  between operations  14.4 us (6%)
  matrix products  6.63 us (3%)
  other arithmetic  6.29 us (3%)
    pallas_call x1, Pallas kernels, project(): pl.pallas_call(functools.partial(fused_kernel, groups, lanes, pad), out_s...  150 us
    pallas_call x1, Pallas kernels, output_projection(): pl.pallas_call(functools.partial(output_kernel, lanes), out_shape=jax.Sha...  38 us
    unnamed x27, local copies, waits for them, and re-layouts  8.15 us
  transfers between devices with their start and end apart: 1, of which 0 were waited for; matrix products, arithmetic and copies ran while one was open for 11% of the time, Pallas kernels for 64%

profile of v1, /device:TPU:9, one launch (start us, length us, event | category | flops | bytes accessed | tf_op | source)
XLA Modules:
  0.0 235.4 jit_solution(2508319795536971405)
XLA Ops:
  6.5 0.0 copy-start
  6.5 0.0 copy-start.3
  6.5 0.0 all-gather.2.cloned.1.call-start
  6.5 1.4 copy-done
  7.9 0.8 constant_dynamic-slice_fusion
  8.7 0.0 all-gather.2.cloned.1.call-update
  8.8 0.7 and_select_fusion
  9.4 0.2 convert_reduce_fusion
  9.6 0.1 iota_add_fusion
  9.7 0.1 add.137
  9.8 0.1 add_add_fusion
  9.9 0.1 add.145
  10.0 0.1 select_reduce_fusion
  10.1 0.1 sub.19
  10.2 0.1 tile.7
  10.3 0.0 copy-start.4
  10.3 0.7 convert_element_type.56
  11.0 0.1 multiply_cosine_fusion
  11.1 3.1 %fusion.28.mods_ref = f32[2,9216]{1,0:T(2,128)S(1)} fusion(bf16[256,9216]{1,0:T(8,128)(2,1)} %param.16, f32[2,128]{1,0:T(2,128)S(1)} %get-tuple-element.14, f32[2,128]{1,0:T(2,128)S(1)} %get-tuple-element.13), kind=kOutput, calls=%fused_computation.60 | convolution fusion | flops 9440256 | bytes 4794368 | tf_op jit(solution)/shard_map/dot_general | solution.py:34
  14.2 0.0 copy-done.3
  14.2 0.0 copy-done.4
  14.2 150.2 %shard_map.109 = (f32[512,1536]{1,0:T(8,128)S(1)}, f32[8,128]{1,0:T(8,128)S(1)}) custom-call(bf16[128,3072]{1,0:T(8,128)(2,1)S(1)} %copy-done.4, s32[8,128]{1,0:T(8,128)S(1)} %broadcast_in_dim.63.place_ref, s32[8,8,128]{2,1,0:T(8,128)S(1)} %broadcast_in_dim.112.tags_ref, f32[2,9216]{1,0:T(2,128)S(1)} %fusion.28.mods_ref, bf16[384,1536]{1,0:T(8,128)(2,1)S(1)} %copy-done.3), custom_call_target="tpu_custom_call" | custom-call | flops 4831838208 | bytes 209715200 | tf_op jit(solution)/shard_map/pallas_call | solution.py:274
  164.4 0.0 copy-start.2
  164.4 1.7 copy-done.2
  166.1 3.5 %copy.25 = f32[512,1536]{0,1:T(8,128)} copy(f32[512,1536]{1,0:T(8,128)} %copy-done.2) | data formatting | bytes 6291456 | tf_op jit(solution)/shard_map/pallas_call | solution.py:274
  169.6 2.3 slice.38
  171.9 0.0 copy-start.10
  171.9 1.6 copy.35
  173.5 0.5 slice.25
  174.7 1.4 reshape.208
  176.1 0.7 fusion.38
  176.8 0.0 copy-start.6
  176.8 0.0 copy-start.9
  176.9 0.8 copy-done.6
  177.6 0.2 multiply_reduce_fusion.1
  177.8 0.0 copy-start.7
  177.9 0.8 copy.38
  178.7 1.8 copy.37
  180.5 0.0 copy-done.10
  180.5 0.0 copy-start.5
  180.5 0.1 compare_bitcast_fusion
  180.6 0.3 fusion.10
  181.0 0.0 copy-start.11
  181.0 1.6 multiply_reduce_fusion
  182.6 0.3 compare_and_fusion
  182.9 0.0 copy-done.7
  183.0 0.0 copy-done.9
  183.0 0.2 multiply_convert_fusion.3
  183.2 0.0 copy-done.5
  183.2 0.1 fusion.22
  183.3 0.3 fusion.12
  183.6 0.0 copy-done.11
  183.6 0.0 copy-start.8
  183.7 2.1 fusion
  185.8 0.0 copy-done.8
  185.8 1.4 divide_convert_fusion
  187.2 0.2 copy.33.mixed_ref
  187.5 0.0 all-gather.2.cloned.1.call-done.weight_ref
  187.5 0.0 copy-start.1
  187.5 1.9 copy-done.1
  189.4 38.0 %shard_map.110 = f32[128,3072]{1,0:T(8,128)S(1)} custom-call(bf16[512,512]{1,0:T(8,128)(2,1)S(1)} %copy.33.mixed_ref, bf16[512,3072]{1,0:T(8,128)(2,1)S(1)} %copy-done.1), custom_call_target="tpu_custom_call" | custom-call | tf_op jit(solution)/shard_map/pallas_call | solution.py:352
  227.4 1.1 multiply_convert_fusion
  (19 shorter events, 0.2 us)
Async XLA Ops:
  6.5 1.4 copy-start
  6.5 7.7 %copy-start.3 = (bf16[384,1536]{1,0:T(8,128)(2,1)S(1)}, bf16[384,1536]{1,0:T(8,128)(2,1)}, u32[]{:S(2)}) copy-start(bf16[384,1536]{1,0:T(8,128)(2,1)} %weight_ref.1) | copy-start | bytes 3538948
  6.5 181.0 %all-gather.2.cloned.1.call-start = ((), (), s32[]{:S(2)}) async-start(), calls=%async_computation | async-start | bytes 3538944 | tf_op jit(solution)/shard_map/all_gather | solution.py:410
  10.3 4.0 %copy-start.4 = (bf16[128,3072]{1,0:T(8,128)(2,1)S(1)}, bf16[128,3072]{1,0:T(8,128)(2,1)}, u32[]{:S(2)}) copy-start(bf16[128,3072]{1,0:T(8,128)(2,1)} %tokens_ref.1) | copy-start | bytes 2359300
  164.4 1.7 copy-start.2
  171.9 8.6 %copy-start.10 = (s32[2]{0:T(128)S(1)}, s32[2]{0:T(128)}, u32[]{:S(2)}) copy-start(s32[2]{0:T(128)} %param.15) | copy-start | bytes 28
  176.8 0.8 copy-start.6
  176.8 6.2 %copy-start.9 = (f32[128]{0:T(128)S(1)}, f32[128]{0:T(128)}, u32[]{:S(2)}) copy-start(f32[128]{0:T(128)} %param.19) | copy-start | bytes 1540
  177.8 5.1 %copy-start.7 = (bf16[2,128,4,1,128]{4,3,2,1,0:T(2,128)(2,1)S(1)}, bf16[2,128,4,1,128]{4,3,2,1,0:T(2,128)(2,1)}, u32[]{:S(2)}) copy-start(bf16[2,128,4,1,128]{4,3,2,1,0:T(2,128)(2,1)} %copy-done.6) | copy-start | bytes 786436
  180.5 2.7 %copy-start.5 = (f32[512,1536]{0,1:T(8,128)S(1)}, f32[512,1536]{0,1:T(8,128)}, u32[]{:S(2)}) copy-start(f32[512,1536]{0,1:T(8,128)} %copy.25) | copy-start | bytes 9437188
  181.0 2.7 %copy-start.11 = (f32[128]{0:T(128)S(1)}, f32[128]{0:T(128)}, u32[]{:S(2)}) copy-start(f32[128]{0:T(128)} %param.18) | copy-start | bytes 1540
  183.6 2.1 copy-start.8
  187.5 1.9 copy-start.1
Sparse Core Ops, SparseCore 0:
  9.4 101.0 all-gather.1

commit v2 on v1

--- a/solution.py
+++ b/solution.py
@@ -32,26 +32,6 @@
     embedded = jnp.concatenate([jnp.cos(angles), jnp.sin(angles)], axis=1)
     active = jax.nn.silu(embedded).astype(jnp.bfloat16)
     return jnp.dot(active, mod_weight, preferred_element_type=jnp.float32)
-
-
-def select_rows(mods, owner):
-    onehot = (owner[:, None] == jnp.arange(mods.shape[0], dtype=jnp.int32)[None, :]).astype(
-        jnp.float32
-    )
-    return jnp.dot(onehot, mods, precision=lax.Precision.HIGHEST)
-
-
-def tile_terms(query, q_owner, keys, values, k_owner, k_live):
-    scores = jnp.einsum(
-        "qhd,khd->hqk", query, keys, preferred_element_type=jnp.float32
-    ) * query.shape[-1] ** (-0.5)
-    match = (q_owner[:, None] == k_owner[None, :]) & k_live[None, :]
-    weights = jnp.where(match[None], jnp.exp(scores), 0.0)
-    total = jnp.sum(weights, axis=2)
-    summed = jnp.einsum(
-        "hqk,khd->qhd", weights.astype(jnp.bfloat16), values, preferred_element_type=jnp.float32
-    )
-    return (total, summed)
 
 
 MESH = pl.DeviceIdType.MESH
@@ -67,8 +47,18 @@
     tags_ref,
     mods_ref,
     weight_ref,
+    gains_ref,
+    text_ref,
+    text_code_ref,
+    out_weight_ref,
+    out_ref,
     acc_ref,
-    count_ref,
+    out_weight_all,
+    text_keys,
+    mixed_ref,
+    own_sum,
+    sending,
+    landing,
     out_blocks,
     in_blocks,
     in_tags,
@@ -85,6 +75,11 @@
     cnt_recv,
     ring_send,
     ring_recv,
+    out_send,
+    out_recv,
+    sum_send,
+    sum_recv,
+    local_sem,
 ):
     g = lax.axis_index("grp")
     u = lax.axis_index("uly")
@@ -93,6 +88,10 @@
     half = columns // 2
     piece = depth // CHUNKS
     span = groups * pad
+    share = out_weight_all.shape[1]
+    out_piece = share // CHUNKS
+    heads = columns // (3 * HD)
+    count = rows * lanes
 
     def group_at(position):
         high = position // (groups // 2)
@@ -103,6 +102,12 @@
     ahead = group_at((position + 1) % groups)
     behind = group_at((position + groups - 1) % groups)
 
+    own_copy = pltpu.make_async_copy(
+        out_weight_ref.at[pl.ds(pl.multiple_of(u * share, share), share), :],
+        out_weight_all.at[g],
+        local_sem,
+    )
+    own_copy.start()
     barrier = pltpu.get_barrier_semaphore()
     for k in range(1, groups):
         pl.semaphore_signal(
@@ -219,6 +224,11 @@
         hidden_copy(k).start()
         count_copy(k).start()
 
+    for head in range(heads):
+        raw = text_ref[:, 2 * head * HD : (2 * head + 1) * HD].astype(jnp.float32)
+        text_keys[head] = rms_scale(raw, gains_ref[1:2, :]).astype(jnp.bfloat16)
+    own_copy.wait()
+
     def pass_on(step):
         for chunk in range(CHUNKS):
             for way in range(2):
@@ -249,7 +259,6 @@
     for k in range(1, lanes):
         hidden_copy(k).wait()
         count_copy(k).wait()
-    count_ref[...] = jnp.sum(counts_all[...], axis=0)
 
     def held(step, carry):
         add_block(step)
@@ -261,29 +270,155 @@
         return carry
 
     lax.fori_loop(0, early + 1, held, 0)
-    lax.fori_loop(early, groups - 1, arriving, 0)
-
-
-def project(tokens, place, tags, mods, qkv_weight, pad):
+    lax.fori_loop(early, groups - 2, arriving, 0)
+
+    reach = (groups // 2, (groups - 1) // 2)
+
+    def out_owner(way, step):
+        if way == 0:
+            return group_at((position + groups - step) % groups)
+        return group_at((position + step) % groups)
+
+    def out_copy(way, chunk, step):
+        place = out_weight_all.at[
+            out_owner(way, step), pl.ds(chunk * out_piece, out_piece), :
+        ]
+        return pltpu.make_async_remote_copy(
+            src_ref=place,
+            dst_ref=place,
+            send_sem=out_send.at[way, chunk, step],
+            recv_sem=out_recv.at[way, chunk, step],
+            device_id=((ahead, behind)[way], u),
+            device_id_type=MESH,
+        )
+
+    def pass_on_out(step):
+        for chunk in range(CHUNKS):
+            for way in range(2):
+                if step < reach[way]:
+                    out_copy(way, chunk, step).wait()
+                    if step + 1 < reach[way]:
+                        out_copy(way, chunk, step + 1).start()
+
+    for chunk in range(CHUNKS):
+        for way in range(2):
+            if reach[way] > 0:
+                out_copy(way, chunk, 0).start()
+    arriving(groups - 2, 0)
+
+    first_tokens = jnp.sum(counts_all[...], axis=0)[0:1, 0:1].astype(jnp.int32)
+    key_owner = (
+        lax.broadcasted_iota(jnp.int32, (1, count), 1) >= first_tokens
+    ).astype(jnp.int32)
+    text_code = text_code_ref[0:1, :]
+    tile = count // 2
+    scaling = HD ** (-0.5)
+    dims = (((1,), (1,)), ((), ()))
+    pieces = 2 * heads
+    done = 0
+    for head in range(heads):
+        base = 3 * head * HD
+        keys = rms_scale(acc_ref[:, base + HD : base + 2 * HD], gains_ref[1:2, :]).astype(
+            jnp.bfloat16
+        )
+        vals = acc_ref[:, base + 2 * HD : base + 3 * HD].astype(jnp.bfloat16)
+        text_vals = text_ref[:, (2 * head + 1) * HD : (2 * head + 2) * HD]
+        for part in range(2):
+            at = part * tile
+            query = rms_scale(acc_ref[at : at + tile, base : base + HD], gains_ref[0:1, :]).astype(
+                jnp.bfloat16
+            )
+            query_owner = (
+                at + lax.broadcasted_iota(jnp.int32, (tile, 1), 0) >= first_tokens
+            ).astype(jnp.int32)
+            scores = lax.dot_general(query, keys, dims, preferred_element_type=jnp.float32)
+            near = jnp.where(query_owner == key_owner, jnp.exp(scores * scaling), 0.0)
+            scores = lax.dot_general(
+                query, text_keys[head], dims, preferred_element_type=jnp.float32
+            )
+            far = jnp.where(query_owner == text_code, jnp.exp(scores * scaling), 0.0)
+            total = jnp.sum(near, axis=1, keepdims=True) + jnp.sum(far, axis=1, keepdims=True)
+            summed = jnp.dot(
+                near.astype(jnp.bfloat16), vals, preferred_element_type=jnp.float32
+            ) + jnp.dot(far.astype(jnp.bfloat16), text_vals, preferred_element_type=jnp.float32)
+            mixed_ref[at : at + tile, head * HD : (head + 1) * HD] = (summed / total).astype(
+                jnp.bfloat16
+            )
+            until = (2 * head + part + 1) * (reach[0] // 2) // pieces
+            while done < until:
+                pass_on_out(done)
+                done += 1
+
+    order = sorted(range(1, lanes), key=lambda k: abs(k - lanes // 2))
+    slots = [(0, 0)]
+    for step in range(1, reach[0] + 1):
+        slots += [(way, step) for way in range(2) if step <= reach[way]]
+
+    def sum_copy(k, index):
+        way, step = slots[index]
+        owner = out_owner(way, step)
+        return pltpu.make_async_remote_copy(
+            src_ref=sending.at[k - 1, owner],
+            dst_ref=landing.at[k - 1, owner],
+            send_sem=sum_send.at[k - 1, index],
+            recv_sem=sum_recv.at[k - 1, index],
+            device_id=(g, (u + k) % lanes),
+            device_id_type=MESH,
+        )
+
+    for index, (way, step) in enumerate(slots):
+        while done < step:
+            pass_on_out(done)
+            done += 1
+        owner = out_owner(way, step)
+        block = out_weight_all[owner]
+        for k in order:
+            peer = pl.multiple_of((u + k) % lanes * rows, rows)
+            sending[k - 1, owner] = jnp.dot(
+                mixed_ref[pl.ds(peer, rows), :], block, preferred_element_type=jnp.float32
+            ).astype(jnp.bfloat16)
+            sum_copy(k, index).start()
+        own_sum[owner] = jnp.dot(mixed_ref[mine, :], block, preferred_element_type=jnp.float32)
+    for index in range(len(slots)):
+        for k in order:
+            sum_copy(k, index).wait()
+    gate = jnp.where(first, mods[0:1, 2 * width :], mods[1:2, 2 * width :])
+    for part in range(groups):
+        sum_here = own_sum[part]
+        for k in order:
+            sum_here += landing[k - 1, part].astype(jnp.float32)
+        here = slice(part * depth, (part + 1) * depth)
+        out_ref[:, here] = (gate[:, here] * sum_here).astype(out_ref.dtype)
+
+
+def sublayer(tokens, place, tags, mods, qkv_weight, gains, text, text_code, out_weight, pad):
     groups = lax.axis_size("grp")
     lanes = lax.axis_size("uly")
     rows, width = tokens.shape
     depth, columns = qkv_weight.shape
+    heads = columns // (3 * HD)
+    share = out_weight.shape[0] // lanes
+    out_columns = out_weight.shape[1]
+    count = rows * lanes
     vmem = pl.BlockSpec(memory_space=pltpu.VMEM)
     dma = pltpu.SemaphoreType.DMA
     return pl.pallas_call(
         functools.partial(fused_kernel, groups, lanes, pad),
-        out_shape=(
-            jax.ShapeDtypeStruct((rows * lanes, columns), jnp.float32),
-            jax.ShapeDtypeStruct((8, 128), jnp.float32),
-        ),
-        in_specs=[vmem] * 5,
-        out_specs=(vmem, vmem),
+        out_shape=jax.ShapeDtypeStruct((rows, width), jnp.bfloat16),
+        in_specs=[vmem] * 8 + [pl.BlockSpec(memory_space=pl.ANY)],
+        out_specs=vmem,
         scratch_shapes=[
+            pltpu.VMEM((count, columns), jnp.float32),
+            pltpu.VMEM((groups, share, out_columns), jnp.bfloat16),
+            pltpu.VMEM((heads, text.shape[0], HD), jnp.bfloat16),
+            pltpu.VMEM((count, heads * HD), jnp.bfloat16),
+            pltpu.VMEM((groups, rows, out_columns), jnp.float32),
+            pltpu.VMEM((lanes - 1, groups, rows, out_columns), jnp.bfloat16),
+            pltpu.VMEM((lanes - 1, groups, rows, out_columns), jnp.bfloat16),
             pltpu.VMEM((groups, pad, width), jnp.bfloat16),
             pltpu.VMEM((groups, pad, width), jnp.bfloat16),
             pltpu.VMEM((groups, 8, groups * pad), jnp.int32),
-            pltpu.VMEM((groups, rows * lanes, depth), jnp.bfloat16),
+            pltpu.VMEM((groups, count, depth), jnp.bfloat16),
             pltpu.VMEM((groups, depth, columns), jnp.bfloat16),
             pltpu.VMEM((lanes, 8, 128), jnp.float32),
             dma((groups,)),
@@ -296,74 +431,16 @@
             dma((lanes,)),
             dma((2, CHUNKS, groups)),
             dma((2, CHUNKS, groups)),
+            dma((2, CHUNKS, groups)),
+            dma((2, CHUNKS, groups)),
+            dma((lanes, groups)),
+            dma((lanes, groups)),
+            dma,
         ],
         compiler_params=pltpu.CompilerParams(
-            collective_id=0, has_side_effects=True, vmem_limit_bytes=48 * 1024 * 1024
+            collective_id=0, has_side_effects=True, vmem_limit_bytes=58 * 1024 * 1024
         ),
-        cost_estimate=pl.CostEstimate(
-            flops=2 * rows * lanes * width * columns,
-            bytes_accessed=200 * 1024 * 1024,
-            transcendentals=0,
-        ),
-    )(tokens, place, tags, mods, qkv_weight)
-
-
-def output_kernel(lanes, mixed_ref, weight_ref, out_ref, sending, landing, send_sem, recv_sem):
-    g = lax.axis_index("grp")
-    u = lax.axis_index("uly")
-    rows = out_ref.shape[0]
-    barrier = pltpu.get_barrier_semaphore()
-    for k in range(1, lanes):
-        pl.semaphore_signal(barrier, inc=1, device_id=(g, (u + k) % lanes), device_id_type=MESH)
-    pl.semaphore_wait(barrier, lanes - 1)
-
-    def part(index):
-        return jnp.dot(
-            mixed_ref[pl.ds(pl.multiple_of(index * rows, rows), rows), :],
-            weight_ref[...],
-            preferred_element_type=jnp.float32,
-        )
-
-    def copy(k):
-        return pltpu.make_async_remote_copy(
-            src_ref=sending.at[k - 1],
-            dst_ref=landing.at[k - 1],
-            send_sem=send_sem.at[k - 1],
-            recv_sem=recv_sem.at[k - 1],
-            device_id=(g, (u + k) % lanes),
-            device_id_type=MESH,
-        )
-
-    order = sorted(range(1, lanes), key=lambda k: abs(k - lanes // 2))
-    for k in order:
-        sending[k - 1] = part((u + k) % lanes).astype(jnp.bfloat16)
-        copy(k).start()
-    out_ref[...] = part(u)
-    for k in order:
-        copy(k).wait()
-        out_ref[...] += landing[k - 1].astype(jnp.float32)
-
-
-def output_projection(mixed, weight):
-    lanes = lax.axis_size("uly")
-    rows = mixed.shape[0] // lanes
-    width = weight.shape[1]
-    vmem = pl.BlockSpec(memory_space=pltpu.VMEM)
-    return pl.pallas_call(
-        functools.partial(output_kernel, lanes),
-        out_shape=jax.ShapeDtypeStruct((rows, width), jnp.float32),
-        in_specs=[vmem] * 2,
-        out_specs=vmem,
-        scratch_shapes=[
-            pltpu.VMEM((lanes - 1, rows, width), jnp.bfloat16),
-            pltpu.VMEM((lanes - 1, rows, width), jnp.bfloat16),
-            pltpu.SemaphoreType.DMA((lanes - 1,)),
-            pltpu.SemaphoreType.DMA((lanes - 1,)),
-        ],
-        compiler_params=pltpu.CompilerParams(
-            collective_id=1, has_side_effects=True, vmem_limit_bytes=40 * 1024 * 1024
-        ),
-    )(mixed, weight)
+    )(tokens, place, tags, mods, qkv_weight, gains, text, text_code, out_weight)
 
 
 def body(
@@ -380,14 +457,12 @@
     out_weight,
 ):
     groups = lax.axis_size("grp")
-    lanes = lax.axis_size("uly")
     rows, width = tokens.shape
     blocks = block_image.shape[0]
     capacity = (blocks + groups - 1) // groups
     pad = (capacity * BLK + 15) // 16 * 16
     span = groups * pad
     g = lax.axis_index("grp")
-    u = lax.axis_index("uly")
     target = block_image // IMG_GRP
     own_image = block_image % IMG_GRP
     index = jnp.arange(blocks, dtype=jnp.int32)
@@ -405,40 +480,15 @@
     tags = jnp.broadcast_to(tags[:, None, :], (groups, 8, span))
     places = jnp.broadcast_to(place[None, :], (8, rows))
 
-    share = out_weight.shape[0] // lanes
-    own_rows = lax.dynamic_slice_in_dim(out_weight, u * share, share, axis=0)
-    out_rows = lax.all_gather(own_rows, "grp", axis=1, tiled=True)
-
     mods = modulation(timestep, mod_weight)
-    projected, count = project(tokens, places, tags, mods, qkv_weight, pad)
-    local_heads = qkv_weight.shape[1] // (3 * HD)
-    group_tokens = rows * lanes
-    projected = projected.reshape(-1, local_heads, 3, HD)
-    query = rms_scale(projected[:, :, 0], q_gain).astype(jnp.bfloat16)
-    keys = rms_scale(projected[:, :, 1], k_gain).astype(jnp.bfloat16)
-    values = projected[:, :, 2].astype(jnp.bfloat16)
-    text = text_kv.reshape(IMG_GRP, TXT, local_heads, 2, HD)
-    text_key = (
-        rms_scale(text[:, :, :, 0].astype(jnp.float32), k_gain)
-        .astype(jnp.bfloat16)
-        .reshape(IMG_GRP * TXT, local_heads, HD)
-    )
-    text_value = text[:, :, :, 1].reshape(IMG_GRP * TXT, local_heads, HD)
-    first_count = count[0, 0].astype(jnp.int32)
-    owner = (jnp.arange(group_tokens, dtype=jnp.int32) >= first_count).astype(jnp.int32)
-    text_owner = jnp.repeat(jnp.arange(IMG_GRP, dtype=jnp.int32), TXT)
-    text_live = jnp.tile(jnp.arange(TXT, dtype=jnp.int32), IMG_GRP) < jnp.repeat(txt_len, TXT)
-    all_keys = jnp.concatenate([keys, text_key], axis=0)
-    all_values = jnp.concatenate([values, text_value], axis=0)
-    k_owner = jnp.concatenate([owner, text_owner])
-    k_live = jnp.concatenate([jnp.ones(owner.shape, bool), text_live])
-    total, summed = tile_terms(query, owner, all_keys, all_values, k_owner, k_live)
-    mixed = (summed / total.T[:, :, None]).astype(jnp.bfloat16)
-    mixed = mixed.reshape(group_tokens, local_heads * HD)
-    projection = output_projection(mixed, out_rows)
-    own_first = (u * rows + jnp.arange(rows, dtype=jnp.int32)) < first_count
-    gate = jnp.where(own_first[:, None], mods[0:1, 2 * width :], mods[1:2, 2 * width :])
-    return (gate * projection).astype(jnp.bfloat16)
+    text = text_kv.reshape(IMG_GRP * TXT, text_kv.shape[2])
+    live = jnp.arange(TXT, dtype=jnp.int32)[None, :] < txt_len[:, None]
+    text_code = jnp.where(live, jnp.arange(IMG_GRP, dtype=jnp.int32)[:, None], -1)
+    text_code = jnp.broadcast_to(text_code.reshape(1, IMG_GRP * TXT), (8, IMG_GRP * TXT))
+    gains = jnp.stack([q_gain, k_gain])
+    return sublayer(
+        tokens, places, tags, mods, qkv_weight, gains, text, text_code, out_weight, pad
+    )
 
 
 def solution(mesh):

time: 236 us -> 181 us (0.77)
  Pallas kernels: 188 us -> 169 us
  local copies, waits for them, and re-layouts: 19.9 us -> 4.2 us
  between operations: 14.4 us -> 0.04 us
  matrix products: 6.63 us -> 3.69 us
  other arithmetic: 6.29 us -> 3.87 us
    pallas_call x2 -> x1, Pallas kernels: 188 us -> 169 us  [sublayer(): pl.pallas_call(functools.partial(fused_kernel, groups, lanes, pad), out_s...]
    unnamed x27 -> x1, local copies, waits for them, and re-layouts: 8.15 us -> 2.06 us
    dot_general x2 -> x0, matrix products: 3.57 us -> none  [the longest x1 2.13 us: tile_terms(): jnp.einsum('qhd,khd->hqk', query, keys, preferred_element_type=jnp.float32)]
    slice x4 -> x0, local copies, waits for them, and re-layouts: 3.56 us -> none  [the longest x1 2.29 us: body(): keys = rms_scale(projected[:, :, 1], k_gain).astype(jnp.bfloat16)]
    pallas_call x1 -> x0, local copies, waits for them, and re-layouts: 3.54 us -> none  [project(): pl.pallas_call(functools.partial(fused_kernel, groups, lanes, pad), out_s...]
  transfers between devices with their start and end apart: 1 -> 0, of which waited for: 0 -> 0; matrix products, arithmetic and copies ran while one was open for 11% -> 0% of each run, Pallas kernels for 64% -> 0%
where the time goes in v2:
time: 181 us
  Pallas kernels  169 us (93%)
  local copies, waits for them, and re-layouts  4.2 us (2%)
  other arithmetic  3.87 us (2%)
  matrix products  3.69 us (2%)
    pallas_call x1, Pallas kernels, sublayer(): pl.pallas_call(functools.partial(fused_kernel, groups, lanes, pad), out_s...  169 us
    dot_general x1, matrix products, modulation(): return jnp.dot(active, mod_weight, preferred_element_type=jnp.float32)  3.69 us

profile of v2, /device:TPU:9, one launch (start us, length us, event | category | flops | bytes accessed | tf_op | source)
XLA Modules:
  0.0 180.8 jit_solution(10515122593417765835)
XLA Ops:
  0.0 0.7 convert_element_type.10
  0.7 0.7 fusion.4
  1.4 1.2 pad_maximum_fusion.1.gains_ref
  2.6 0.1 multiply_cosine_fusion
  2.7 0.7 and_select_fusion
  3.4 0.2 convert_reduce_fusion
  3.6 0.1 add_add_fusion
  3.7 0.1 add.102
  3.8 0.6 broadcast_in_dim.76.text_code_ref
  4.4 0.1 iota_add_fusion
  4.5 0.1 add.94
  4.5 0.1 select_reduce_fusion
  4.7 0.1 sub.19
  4.7 0.6 broadcast_in_dim.38.place_ref
  5.3 0.1 tile.9
  5.4 0.6 broadcast_in_dim.47.tags_ref
  6.0 3.7 %fusion.2.mods_ref = f32[2,9216]{1,0:T(2,128)} fusion(bf16[256,9216]{1,0:T(8,128)(2,1)} %param.16, f32[2,128]{1,0:T(2,128)S(1)} %get-tuple-element.6, f32[2,128]{1,0:T(2,128)S(1)} %get-tuple-element.5), kind=kOutput, calls=%fused_computation.20 | convolution fusion | flops 9440256 | bytes 4794368 | tf_op jit(solution)/shard_map/dot_general | solution.py:34
  9.7 169.0 %shard_map.109 = bf16[128,3072]{1,0:T(8,128)(2,1)} custom-call(bf16[128,3072]{1,0:T(8,128)(2,1)} %tokens_ref.1, s32[8,128]{1,0:T(8,128)} %broadcast_in_dim.38.place_ref, s32[8,8,128]{2,1,0:T(8,128)} %broadcast_in_dim.47.tags_ref, f32[2,9216]{1,0:T(2,128)} %fusion.2.mods_ref, bf16[384,1536]{1,0:T(8,128)(2,1)} %weight_ref.1, ...), custom_call_target="tpu_custom_call" | custom-call | tf_op jit(solution)/shard_map/pallas_call | solution.py:405
  178.8 2.1 %copy.13 = bf16[128,3072]{1,0:T(8,128)(2,1)} copy(bf16[128,3072]{1,0:T(8,128)(2,1)} %shard_map.109) | data formatting | bytes 1572864
  (6 shorter events, 0.0 us)
